TPU v7x, 32 devices: a whole 2x2x4 slice. The times are simulated.
32 devices in a mesh: row: 4 (over y, x), col: 8 (over z, core).
Axes of the slice: x: 2, y: 2, z: 4, core: 2. Of those that a mesh axis runs over, the one named last changes fastest.
Arguments:
- latent: bfloat16 [64, 64, 256], P('row', 'col'), may hold values from -6 to 6
- well_logs: bfloat16 [32, 256], P(('row', 'col')), may hold values from -6 to 6
- cond_weight: bfloat16 [256, 256], replicated, may hold values from -0.375 to 0.375
- trace_rows: int32 [64], P('col'), may hold values from 0 to 31, as said below
- norm_gain: float32 [256], replicated, may hold values from 0.5 to 1.5
- in_weight: bfloat16 [256, 512], replicated, may hold values from -0.375 to 0.375
- conv_weight: float32 [9, 256], replicated, may hold values from -2 to 2
- bc_weight: bfloat16 [256, 1024], replicated, may hold values from -0.375 to 0.375
- dt_weight: bfloat16 [256, 64], replicated, may hold values from -0.375 to 0.375
- dt_bias: float32 [4, 16], replicated, may hold values from -0.5 to 0.5
- row_rate: float32 [2, 16], replicated, may hold values from 1 to 512
- col_rate: float32 [2, 16], replicated, may hold values from 1 to 512
- horizon: float32 [64, 64], P('row', 'col'), may hold values from 0 to 1
- out_gain: float32 [256], replicated, may hold values from 0.5 to 1.5
- out_weight: bfloat16 [256, 256], replicated, may hold values from -0.375 to 0.375
Outputs:
- block_out: bfloat16 [64, 64, 256], P('row', 'col')
Inputs may be any that keep to these rules, and one draw needn't show every extreme that they name: `trace_rows`: every conditioning token row is named by some plane column.
All inputs are finite; a program needn't handle non-finite values.
Results may differ from a plain program's by a relative error of at most 0.009.
Values may be sent and summed in bfloat16 or wider, within the bound.
A program may use at most 192 MiB of HBM per device.

v0:
```python
import functools

import jax
import jax.numpy as jnp
from jax import lax
from jax.experimental import pallas as pl
from jax.experimental.pallas import tpu as pltpu
from jax.sharding import PartitionSpec as P

MESH = pl.DeviceIdType.MESH
F32 = jnp.float32
BF16 = jnp.bfloat16
VMEM_LIMIT = 64 * 1024 * 1024


def exact_dot(a, b):
    return jnp.dot(a, b, preferred_element_type=F32, precision=lax.Precision.HIGHEST)


def dot(a, b):
    return jnp.dot(a.astype(BF16), b.astype(BF16), preferred_element_type=F32)


def dot_t(a, b):
    return lax.dot_general(
        a.astype(BF16), b.astype(BF16), (((1,), (1,)), ((), ())), preferred_element_type=F32
    )


def dot_first(a, b):
    return lax.dot_general(
        a.astype(BF16), b.astype(BF16), (((0,), (0,)), ((), ())), preferred_element_type=F32
    )


def split_dot(a, ones):
    high = a.astype(BF16)
    low = (a - high.astype(F32)).astype(BF16)
    both = jnp.dot(jnp.concatenate([high, low], axis=0), ones, preferred_element_type=F32)
    return both[: a.shape[0]] + both[a.shape[0] :]


def silu(v):
    return v / (1.0 + jnp.exp(-v))


def softplus(v):
    return jnp.maximum(v, 0.0) + jnp.log1p(jnp.exp(-jnp.abs(v)))


def kernel(
    n_row,
    n_col,
    *refs,
):
    hbm, out_ref, own = refs[:15], refs[15], refs[16:31]
    (
        latent_ref,
        logs_ref,
        cond_ref,
        trace_ref,
        norm_gain_ref,
        in_ref,
        conv_ref,
        bc_ref,
        dt_ref,
        dt_bias_ref,
        row_rate_ref,
        col_rate_ref,
        horizon_ref,
        out_gain_ref,
        out_weight_ref,
    ) = own
    (
        load_sem,
        shifts,
        lat_f,
        logs_f,
        logs_all,
        logs_flat,
        picks,
        picks_side,
        edge_out,
        edge_line,
        edge_side,
        hz_row,
        hz_col,
        strip_row,
        strip_col,
        logs_send,
        logs_recv,
        edge_send,
        edge_recv,
        hz_send_r,
        hz_recv_r,
        hz_send_c,
        hz_recv_c,
        mix_send_r,
        mix_recv_r,
        pass_send,
        pass_recv,
        mix_send_c,
        mix_recv_c,
    ) = refs[31:]
    rows, cols, width = latent_ref.shape
    cells = rows * cols
    count = n_row * n_col
    inner = in_ref.shape[1] // 2
    heads = dt_bias_ref.shape[1]
    head_dim = inner // heads
    state = bc_ref.shape[1] // 8
    lanes = 4 * heads
    r = lax.axis_index("row")
    c = lax.axis_index("col")
    me = r * n_col + c
    n_token = logs_all.shape[0] * logs_all.shape[1]
    up, down = lax.rem(r + n_row - 1, n_row), lax.rem(r + 1, n_row)
    left, right = lax.rem(c + n_col - 1, n_col), lax.rem(c + 1, n_col)

    barrier = pltpu.get_barrier_semaphore()

    loads = [
        pltpu.make_async_copy(hbm[k], own[k], load_sem.at[k]) for k in range(len(hbm))
    ]
    for k in (0, 1, 12, 3, 2, 5, 4, 6, 7, 8, 9, 10, 11, 13, 14):
        loads[k].start()

    def greet(o, carry):
        d = lax.rem(me + o, count)
        pl.semaphore_signal(
            barrier, inc=1, device_id=(d // n_col, lax.rem(d, n_col)), device_id_type=MESH
        )
        return carry

    lax.fori_loop(1, count, greet, 0)

    for k in (0, 1, 3, 12):
        loads[k].wait()
    lat = latent_ref[...].astype(F32)
    lat_f[...] = lat
    edge_out[0] = lat_f[:, 0, :]
    edge_out[1] = lat_f[:, cols - 1, :]
    logs_f[...] = logs_ref[...].astype(F32)
    logs_all[me] = logs_f[...]
    sub = lax.broadcasted_iota(jnp.int32, (cols, n_token), 0)
    lane = lax.broadcasted_iota(jnp.int32, (cols, n_token), 1)
    want = jnp.zeros((cols, n_token), jnp.int32)
    for j in range(cols):
        want = jnp.where(sub == j, trace_ref[j], want)
    picks[...] = (want == lane).astype(F32)
    line_pick = (
        lax.broadcasted_iota(jnp.int32, (rows, cells), 1) // cols
        == lax.broadcasted_iota(jnp.int32, (rows, cells), 0)
    ).astype(F32)
    column_pick = lax.rem(
        lax.broadcasted_iota(jnp.int32, (cols, cells), 1), cols
    ) == lax.broadcasted_iota(jnp.int32, (cols, cells), 0)
    marks = jnp.sum(
        jnp.where(column_pick, exact_dot(horizon_ref[...], line_pick), 0.0), axis=0, keepdims=True
    )
    hz_row[c] = marks
    hz_col[r] = marks

    pl.semaphore_wait(barrier, count - 1)

    def logs_copy(o):
        d = lax.rem(me + o, count)
        return pltpu.make_async_remote_copy(
            src_ref=logs_f,
            dst_ref=logs_all.at[me],
            send_sem=logs_send.at[o],
            recv_sem=logs_recv.at[o],
            device_id=(d // n_col, lax.rem(d, n_col)),
            device_id_type=MESH,
        )

    def start_logs(o, carry):
        logs_copy(o).start()
        return carry

    lax.fori_loop(1, count, start_logs, 0)

    last = rows - 1
    edges = []
    for src, dst, to in (
        (picks, picks_side.at[0], (r, right)),
        (picks, picks_side.at[1], (r, left)),
        (edge_out.at[1], edge_side.at[0], (r, right)),
        (edge_out.at[0], edge_side.at[1], (r, left)),
        (lat_f.at[last], edge_line.at[0], (down, c)),
        (lat_f.at[last], edge_line.at[1], (down, right)),
        (lat_f.at[last], edge_line.at[2], (down, left)),
        (lat_f.at[0], edge_line.at[3], (up, c)),
        (lat_f.at[0], edge_line.at[4], (up, right)),
        (lat_f.at[0], edge_line.at[5], (up, left)),
    ):
        k = len(edges)
        edges.append(
            pltpu.make_async_remote_copy(
                src_ref=src,
                dst_ref=dst,
                send_sem=edge_send.at[k],
                recv_sem=edge_recv.at[k],
                device_id=to,
                device_id_type=MESH,
            )
        )
        edges[-1].start()

    def fan(buffer, place, n, axis, send, recv, step):
        copies = []
        for o in range(step, n, step):
            to = lax.rem(place + o, n)
            copies.append(
                pltpu.make_async_remote_copy(
                    src_ref=buffer.at[place],
                    dst_ref=buffer.at[place],
                    send_sem=send.at[o],
                    recv_sem=recv.at[o],
                    device_id=(to, c) if axis == 0 else (r, to),
                    device_id_type=MESH,
                )
            )
            copies[-1].start()
        return copies

    hz_copies = fan(hz_row, c, n_col, 1, hz_send_r, hz_recv_r, 1)
    hz_copies += fan(hz_col, r, n_row, 0, hz_send_c, hz_recv_c, 1)

    lane_head = lax.rem(lax.broadcasted_iota(jnp.int32, (lanes, heads), 0), heads)
    spread = (lane_head == lax.broadcasted_iota(jnp.int32, (lanes, heads), 1)).astype(F32)

    def lane_column(table, first):
        wide = lax.dot_general(
            spread,
            table,
            (((1,), (1,)), ((), ())),
            preferred_element_type=F32,
            precision=lax.Precision.HIGHEST,
        )
        kind = lax.broadcasted_iota(jnp.int32, wide.shape, 0) // heads
        own = lax.broadcasted_iota(jnp.int32, wide.shape, 1) + first
        return jnp.sum(jnp.where(kind == own, wide, 0.0), axis=1, keepdims=True)

    for k in (9, 10, 11):
        loads[k].wait()
    bias = lane_column(dt_bias_ref[...], 0)
    rates = lane_column(row_rate_ref[...] / (16.0 * cols * n_col), 0) + lane_column(
        col_rate_ref[...] / (16.0 * rows * n_row), 2
    )
    expand = (
        lax.broadcasted_iota(jnp.int32, (heads, inner), 0)
        == lax.broadcasted_iota(jnp.int32, (heads, inner), 1) // head_dim
    ).astype(BF16)

    cell_0 = lax.broadcasted_iota(jnp.int32, (cells, cells), 0)
    cell_1 = lax.broadcasted_iota(jnp.int32, (cells, cells), 1)
    i0, j0 = cell_0 // cols, lax.rem(cell_0, cols)
    i1, j1 = cell_1 // cols, lax.rem(cell_1, cols)

    n_src = cells + 6 * cols + 2 * rows
    src_id = lax.broadcasted_iota(jnp.int32, (cells, n_src), 1)
    cell_id = lax.broadcasted_iota(jnp.int32, (cells, 1), 0)
    ci, cj = cell_id // cols, lax.rem(cell_id, cols)
    for a in range(3):
        for b in range(3):
            pi, pj = ci + a - 1, cj + b - 1
            row_in = (pi >= 0) & (pi < rows)
            where_from = pi * cols + pj
            line_base = jnp.where(pi < 0, cells, cells + 3 * cols)
            line_from = line_base + jnp.where(
                pj < 0, 2 * cols - 1, jnp.where(pj >= cols, 2 * cols, pj)
            )
            side_from = cells + 6 * cols + pi + jnp.where(pj < 0, 0, rows)
            source = jnp.where(
                row_in, jnp.where((pj >= 0) & (pj < cols), where_from, side_from), line_from
            )
            gi, gj = r * rows + pi, c * cols + pj
            inside = (gi >= 0) & (gi < n_row * rows) & (gj >= 0) & (gj < n_col * cols)
            source = jnp.where(inside, source, -1)
            shifts[3 * a + b] = (src_id == source).astype(BF16)

    def wait_logs(o, carry):
        logs_copy(o).wait()
        return carry

    lax.fori_loop(1, count, wait_logs, 0)
    per = logs_all.shape[1]
    for k in range(logs_all.shape[0]):
        logs_flat[pl.ds(k * per, per), :] = logs_all[k]
    loads[2].wait()
    tokens = silu(dot(logs_flat[...], cond_ref[...])).astype(BF16)

    for edge in edges:
        edge.wait()
    own_tokens = dot(picks[...], tokens)
    left_tokens = dot(picks_side[0], tokens)
    right_tokens = dot(picks_side[1], tokens)

    hidden_own = (lat_f[...] + own_tokens[None]).reshape(cells, width)
    left_token = left_tokens[cols - 1 : cols]
    right_token = right_tokens[0:1]
    hidden = jnp.concatenate(
        [
            hidden_own,
            edge_line[0] + own_tokens,
            edge_line[1] + left_tokens,
            edge_line[2] + right_tokens,
            edge_line[3] + own_tokens,
            edge_line[4] + left_tokens,
            edge_line[5] + right_tokens,
            edge_side[0] + left_token,
            edge_side[1] + right_token,
        ],
        axis=0,
    )
    for k in (4, 5, 6):
        loads[k].wait()
    normed = (
        hidden
        * lax.rsqrt(jnp.mean(hidden * hidden, axis=-1, keepdims=True) + 1e-06)
        * norm_gain_ref[...]
    ).astype(BF16)
    pre_conv = dot(normed, in_ref[:, :inner]).astype(BF16)
    gate_part = dot(normed[:cells], in_ref[:, inner:]).astype(BF16)
    conv_sum = jnp.zeros((cells, inner), F32)
    for k in range(9):
        conv_sum = conv_sum + dot(shifts[k], pre_conv) * conv_ref[k : k + 1, :]
    mixed = silu(conv_sum).astype(BF16)
    strip_row[c] = mixed
    strip_col[r] = mixed
    sibling = c + 1 - 2 * lax.rem(c, 2)

    def to_sibling(e):
        place = lax.rem(c + n_col - 2 * e, n_col)
        return pltpu.make_async_remote_copy(
            src_ref=strip_row.at[place],
            dst_ref=strip_row.at[place],
            send_sem=pass_send.at[e],
            recv_sem=pass_recv.at[e],
            device_id=(r, sibling),
            device_id_type=MESH,
        )

    row_copies = fan(strip_row, c, n_col, 1, mix_send_r, mix_recv_r, 2)
    col_copies = fan(strip_col, r, n_row, 0, mix_send_c, mix_recv_c, 1)
    passed = [to_sibling(e) for e in range(n_col // 2)]
    passed[0].start()

    mixed_f = mixed.astype(F32)
    loads[7].wait()
    loads[8].wait()
    coefs = dot(mixed, bc_ref[...]).astype(BF16)
    in_coef = [coefs[:, 2 * k * state : (2 * k + 1) * state] for k in range(4)]
    out_coef = [coefs[:, (2 * k + 1) * state : (2 * k + 2) * state] for k in range(4)]

    def steps_of(x, marks, first, last):
        step = softplus(dot_t(dt_ref[first:last, :], x) + bias[first:last])
        return step, -step * rates[first:last] - marks

    step, decay = steps_of(mixed, marks, 0, lanes)
    total = jnp.zeros((cells, inner), F32)
    entry = []
    for k in range(4):
        if k < 2:
            same, p0, p1, length = i0 == i1, j0, j1, cols
        else:
            same, p0, p1, length = j0 == j1, i0, i1, rows
        if k % 2 == 1:
            p0, p1 = length - 1 - p0, length - 1 - p1
        halves = []
        while length > 1:
            length //= 2
            halves.append(length)
        reach = []
        for half in halves:
            block = (p0 // half) == (p1 // half)
            late = lax.rem(p1 // half, 2) == 1
            reach.append(same & block & ((late & (p0 <= p1)) | (~late & (p0 > p1))))
        reach.append(same & (p0 <= p1))
        sums = split_dot(
            decay[k * heads : (k + 1) * heads],
            jnp.concatenate([one.astype(BF16) for one in reach], axis=1),
        )
        own_step = step[k * heads : (k + 1) * heads]
        factor = jnp.exp(sums)
        wide = dot_first(
            jnp.concatenate(
                [factor.astype(BF16), (factor * jnp.tile(own_step, (1, len(reach)))).astype(BF16)]
                + [own_step.astype(BF16)],
                axis=1,
            ),
            expand,
        )
        wide = [wide[n * cells : (n + 1) * cells] for n in range(2 * len(reach) + 1)]
        scores = dot_t(out_coef[k], in_coef[k])
        total = total + dot(jnp.where(cell_0 == cell_1, scores, 0.0), mixed_f * wide[-1])
        for n, half in enumerate(halves):
            b0, b1 = p0 // half, p1 // half
            pair = same & (b0 == b1 + 1) & (lax.rem(b0, 2) == 1)
            total = total + wide[n] * dot(
                jnp.where(pair, scores, 0.0), mixed_f * wide[len(reach) + n]
            )
        entry.append(wide[len(halves)])

    def entering(first, strip, marks, place, n, same, later):
        after = (same & (later > 0)).astype(BF16)
        before = (same & (later < 0)).astype(BF16)
        whole = same.astype(BF16)
        x_all = strip[...].reshape(n * cells, inner)
        marks = jnp.concatenate([marks[q] for q in range(n)], axis=1)
        step, decay = steps_of(x_all, marks, first * heads, (first + 2) * heads)
        tile = [slice(q * cells, (q + 1) * cells) for q in range(n)]

        def stacked(part, ones):
            sums = split_dot(
                jnp.concatenate([part[:, tile[q]] for q in range(n)], axis=0),
                jnp.concatenate([ones, whole], axis=1),
            )
            sums = [sums[q * heads : (q + 1) * heads] for q in range(n)]
            return [one[:, :cells] for one in sums], [one[:, cells:] for one in sums]

        sums_f, totals_f = stacked(decay[:heads], after)
        sums_b, totals_b = stacked(decay[heads:], before)
        carry = jnp.zeros((heads, cells), F32)
        for q in reversed(range(n)):
            sums_f[q] = sums_f[q] + carry
            carry = carry + jnp.where(q < place, totals_f[q], 0.0)
        carry = jnp.zeros((heads, cells), F32)
        for q in range(n):
            sums_b[q] = sums_b[q] + carry
            carry = carry + jnp.where(q > place, totals_b[q], 0.0)
        gains = []
        for q in range(n):
            gain = jnp.where(q < place, step[:heads, tile[q]], step[heads:, tile[q]])
            gain = gain * jnp.exp(jnp.where(q < place, sums_f[q], sums_b[q]))
            gains.append(jnp.where(q == place, 0.0, gain))
        wide = dot_first(jnp.concatenate(gains, axis=1), expand)
        weight_f = bc_ref[:, 2 * first * state : (2 * first + 1) * state]
        weight_b = bc_ref[:, (2 * first + 2) * state : (2 * first + 3) * state]
        inflow = jnp.zeros((cells, inner), F32)
        for q in range(n):
            ahead = q < place
            x = x_all[tile[q]]
            driven = x.astype(F32) * wide[tile[q]]
            coef = dot(x, jnp.where(ahead, weight_f, weight_b))
            reader = jnp.where(ahead, out_coef[first], out_coef[first + 1])
            scores = jnp.where(same, dot_t(reader, coef), 0.0)
            inflow = inflow + jnp.where(ahead, entry[first], entry[first + 1]) * dot(
                scores, driven
            )
        return inflow

    for copy in hz_copies:
        copy.wait()
    for e, copy in enumerate(row_copies):
        copy.wait()
        passed[e + 1].start()
    for copy in col_copies:
        copy.wait()
    total = total + entering(2, strip_col, hz_col, r, n_row, j0 == j1, i0 - i1)
    for copy in passed:
        copy.wait()
    total = total + entering(0, strip_row, hz_row, c, n_col, i0 == i1, j0 - j1)

    loads[13].wait()
    loads[14].wait()
    gated = (
        total
        * lax.rsqrt(jnp.mean(total * total, axis=-1, keepdims=True) + 1e-05)
        * out_gain_ref[...]
        * silu(gate_part.astype(F32))
    ).astype(BF16)
    result = hidden_own + dot(gated, out_weight_ref[...])
    out_ref[...] = result.reshape(rows, cols, width).astype(BF16)


def per_device(n_row, n_col, *args):
    (
        latent,
        logs,
        cond,
        trace,
        norm_gain,
        in_weight,
        conv,
        bc,
        dt,
        dt_bias,
        row_rate,
        col_rate,
        horizon,
        out_gain,
        out_weight,
    ) = args
    rows, cols, width = latent.shape
    inner = in_weight.shape[1] // 2
    cells = rows * cols
    count = n_row * n_col
    per = logs.shape[0]
    vmem = pl.BlockSpec(memory_space=pltpu.VMEM)
    operands = (
        latent,
        logs,
        cond,
        trace,
        norm_gain.reshape(1, width),
        in_weight,
        conv,
        bc,
        dt.T,
        dt_bias,
        row_rate,
        col_rate,
        horizon.T,
        out_gain.reshape(1, inner),
        out_weight,
    )
    own = [pltpu.VMEM(one.shape, one.dtype) for one in operands]
    own[3] = pltpu.SMEM(trace.shape, trace.dtype)
    dma = pltpu.SemaphoreType.DMA
    return pl.pallas_call(
        functools.partial(kernel, n_row, n_col),
        out_shape=jax.ShapeDtypeStruct((rows, cols, width), BF16),
        in_specs=[pl.BlockSpec(memory_space=pltpu.HBM)] * len(operands),
        out_specs=vmem,
        scratch_shapes=own
        + [
            dma((len(operands),)),
            pltpu.VMEM((9, cells, cells + 6 * cols + 2 * rows), BF16),
            pltpu.VMEM((rows, cols, width), F32),
            pltpu.VMEM((per, width), F32),
            pltpu.VMEM((count, per, width), F32),
            pltpu.VMEM((count * per, width), F32),
            pltpu.VMEM((cols, count * per), F32),
            pltpu.VMEM((2, cols, count * per), F32),
            pltpu.VMEM((2, rows, width), F32),
            pltpu.VMEM((6, cols, width), F32),
            pltpu.VMEM((2, rows, width), F32),
            pltpu.VMEM((n_col, 1, cells), F32),
            pltpu.VMEM((n_row, 1, cells), F32),
            pltpu.VMEM((n_col, cells, inner), BF16),
            pltpu.VMEM((n_row, cells, inner), BF16),
            dma((count,)),
            dma((count,)),
            dma((10,)),
            dma((10,)),
            dma((n_col,)),
            dma((n_col,)),
            dma((n_row,)),
            dma((n_row,)),
            dma((n_col,)),
            dma((n_col,)),
            dma((n_col // 2,)),
            dma((n_col // 2,)),
            dma((n_row,)),
            dma((n_row,)),
        ],
        compiler_params=pltpu.CompilerParams(
            collective_id=0, has_side_effects=True, vmem_limit_bytes=VMEM_LIMIT
        ),
    )(*operands)


def solution(mesh):
    placed = (
        P("row", "col", None),
        P(("row", "col"), None),
        P(),
        P("col"),
        P(),
        P(),
        P(),
        P(),
        P(),
        P(),
        P(),
        P(),
        P("row", "col"),
        P(),
        P(),
    )
    return jax.shard_map(
        functools.partial(per_device, mesh.shape["row"], mesh.shape["col"]),
        mesh=mesh,
        in_specs=placed,
        out_specs=P("row", "col", None),
        check_vma=False,
    )
```

profile of v0, /device:TPU:0, one launch (start us, length us, event | category | flops | bytes accessed | tf_op | source)
XLA Modules:
  0.0 26.5 jit_solution(1255053654767578885)
XLA Ops:
  0.0 25.0 %shard_map.145 = bf16[16,8,256]{2,1,0:T(8,128)(2,1)} custom-call(bf16[16,8,256]{2,1,0:T(8,128)(2,1)} %refs_0_.1, bf16[1,256]{1,0:T(2,128)(2,1)} %refs_1_.1, bf16[256,256]{1,0:T(8,128)(2,1)} %refs_2_.1, s32[8]{0:T(128)} %refs_3_.1, f32[1,256]{1,0:T(1,128)} %bitcast.6, bf16[256,512]{1,0:T(8,128)(2,1)} %refs_5_.1, f32[9,256]{1,0:T(8,128)} %refs_6_.1, ...), custom_call_target="tpu_custom_call" | custom-call | tf_op jit(solution)/shard_map/pallas_call | solution.py:522
  25.0 1.5 %copy.17 = bf16[16,8,256]{2,1,0:T(8,128)(2,1)} copy(bf16[16,8,256]{2,1,0:T(8,128)(2,1)} %shard_map.145) | data formatting | bytes 131072
where the time goes:
time: 26.7 us; the launch traced here: 26.5 us
  Pallas kernels  25 us (94%)
  local copies, waits for them, and re-layouts  1.47 us (6%)
    pallas_call x1, Pallas kernels, per_device(): pl.pallas_call(functools.partial(kernel, n_row, n_col), out_shape=jax.Sha...  25 us
    unnamed x1, local copies, waits for them, and re-layouts  1.47 us

commit v1 on v0

--- a/solution.py
+++ b/solution.py
@@ -125,14 +125,13 @@
     for k in (0, 1, 12, 3, 2, 5, 4, 6, 7, 8, 9, 10, 11, 13, 14):
         loads[k].start()
 
-    def greet(o, carry):
-        d = lax.rem(me + o, count)
+    row_of = [lax.rem(r + o, n_row) for o in range(n_row)]
+    col_of = [lax.rem(c + o, n_col) for o in range(n_col)]
+    others = [(i, j) for i in range(n_row) for j in range(n_col) if i + j > 0]
+    for i, j in others:
         pl.semaphore_signal(
-            barrier, inc=1, device_id=(d // n_col, lax.rem(d, n_col)), device_id_type=MESH
-        )
-        return carry
-
-    lax.fori_loop(1, count, greet, 0)
+            barrier, inc=1, device_id=(row_of[i], col_of[j]), device_id_type=MESH
+        )
 
     for k in (0, 1, 3, 12):
         loads[k].wait()
@@ -163,22 +162,15 @@
 
     pl.semaphore_wait(barrier, count - 1)
 
-    def logs_copy(o):
-        d = lax.rem(me + o, count)
-        return pltpu.make_async_remote_copy(
+    for i, j in others:
+        pltpu.make_async_remote_copy(
             src_ref=logs_f,
             dst_ref=logs_all.at[me],
-            send_sem=logs_send.at[o],
-            recv_sem=logs_recv.at[o],
-            device_id=(d // n_col, lax.rem(d, n_col)),
+            send_sem=logs_send,
+            recv_sem=logs_recv,
+            device_id=(row_of[i], col_of[j]),
             device_id_type=MESH,
-        )
-
-    def start_logs(o, carry):
-        logs_copy(o).start()
-        return carry
-
-    lax.fori_loop(1, count, start_logs, 0)
+        ).start()
 
     last = rows - 1
     edges = []
@@ -280,11 +272,12 @@
             source = jnp.where(inside, source, -1)
             shifts[3 * a + b] = (src_id == source).astype(BF16)
 
-    def wait_logs(o, carry):
-        logs_copy(o).wait()
-        return carry
-
-    lax.fori_loop(1, count, wait_logs, 0)
+    def wait_for(part, sem):
+        pltpu.make_async_copy(part, part, sem).wait()
+
+    arrived = logs_all.at[pl.ds(0, count - 1)]
+    wait_for(arrived, logs_recv)
+    wait_for(arrived, logs_send)
     per = logs_all.shape[1]
     for k in range(logs_all.shape[0]):
         logs_flat[pl.ds(k * per, per), :] = logs_all[k]
@@ -383,72 +376,76 @@
             jnp.concatenate([one.astype(BF16) for one in reach], axis=1),
         )
         own_step = step[k * heads : (k + 1) * heads]
-        factor = jnp.exp(sums)
+        factor = jnp.exp(sums[:, : len(halves) * cells])
         wide = dot_first(
             jnp.concatenate(
-                [factor.astype(BF16), (factor * jnp.tile(own_step, (1, len(reach)))).astype(BF16)]
-                + [own_step.astype(BF16)],
-                axis=1,
+                [factor, factor * jnp.tile(own_step, (1, len(halves))), own_step], axis=1
             ),
             expand,
         )
-        wide = [wide[n * cells : (n + 1) * cells] for n in range(2 * len(reach) + 1)]
+        wide = [wide[n * cells : (n + 1) * cells] for n in range(2 * len(halves) + 1)]
         scores = dot_t(out_coef[k], in_coef[k])
         total = total + dot(jnp.where(cell_0 == cell_1, scores, 0.0), mixed_f * wide[-1])
         for n, half in enumerate(halves):
             b0, b1 = p0 // half, p1 // half
             pair = same & (b0 == b1 + 1) & (lax.rem(b0, 2) == 1)
             total = total + wide[n] * dot(
-                jnp.where(pair, scores, 0.0), mixed_f * wide[len(reach) + n]
+                jnp.where(pair, scores, 0.0), mixed_f * wide[len(halves) + n]
             )
-        entry.append(wide[len(halves)])
-
-    def entering(first, strip, marks, place, n, same, later):
+        entry.append(sums[:, len(halves) * cells :])
+
+    def entering(first, strip, marks, place, tiles, same, later):
         after = (same & (later > 0)).astype(BF16)
         before = (same & (later < 0)).astype(BF16)
         whole = same.astype(BF16)
-        x_all = strip[...].reshape(n * cells, inner)
-        marks = jnp.concatenate([marks[q] for q in range(n)], axis=1)
-        step, decay = steps_of(x_all, marks, first * heads, (first + 2) * heads)
-        tile = [slice(q * cells, (q + 1) * cells) for q in range(n)]
+        n = len(tiles)
+        xs = [strip[q] for q in tiles]
+        marks = jnp.concatenate([marks[q] for q in tiles], axis=1)
+        step, decay = steps_of(
+            jnp.concatenate(xs, axis=0), marks, first * heads, (first + 2) * heads
+        )
+        tile = [slice(m * cells, (m + 1) * cells) for m in range(n)]
 
         def stacked(part, ones):
             sums = split_dot(
-                jnp.concatenate([part[:, tile[q]] for q in range(n)], axis=0),
+                jnp.concatenate([part[:, tile[m]] for m in range(n)], axis=0),
                 jnp.concatenate([ones, whole], axis=1),
             )
-            sums = [sums[q * heads : (q + 1) * heads] for q in range(n)]
+            sums = [sums[m * heads : (m + 1) * heads] for m in range(n)]
             return [one[:, :cells] for one in sums], [one[:, cells:] for one in sums]
 
         sums_f, totals_f = stacked(decay[:heads], after)
         sums_b, totals_b = stacked(decay[heads:], before)
-        carry = jnp.zeros((heads, cells), F32)
-        for q in reversed(range(n)):
-            sums_f[q] = sums_f[q] + carry
-            carry = carry + jnp.where(q < place, totals_f[q], 0.0)
-        carry = jnp.zeros((heads, cells), F32)
-        for q in range(n):
-            sums_b[q] = sums_b[q] + carry
-            carry = carry + jnp.where(q > place, totals_b[q], 0.0)
         gains = []
-        for q in range(n):
-            gain = jnp.where(q < place, step[:heads, tile[q]], step[heads:, tile[q]])
-            gain = gain * jnp.exp(jnp.where(q < place, sums_f[q], sums_b[q]))
-            gains.append(jnp.where(q == place, 0.0, gain))
+        for m, q in enumerate(tiles):
+            gain = jnp.where(q < place, step[:heads, tile[m]], step[heads:, tile[m]])
+            gains.append(gain * jnp.exp(jnp.where(q < place, sums_f[m], sums_b[m])))
         wide = dot_first(jnp.concatenate(gains, axis=1), expand)
         weight_f = bc_ref[:, 2 * first * state : (2 * first + 1) * state]
         weight_b = bc_ref[:, (2 * first + 2) * state : (2 * first + 3) * state]
-        inflow = jnp.zeros((cells, inner), F32)
-        for q in range(n):
+        out = []
+        for m, q in enumerate(tiles):
             ahead = q < place
-            x = x_all[tile[q]]
-            driven = x.astype(F32) * wide[tile[q]]
-            coef = dot(x, jnp.where(ahead, weight_f, weight_b))
+            driven = xs[m].astype(F32) * wide[tile[m]]
+            coef = dot(xs[m], jnp.where(ahead, weight_f, weight_b))
             reader = jnp.where(ahead, out_coef[first], out_coef[first + 1])
             scores = jnp.where(same, dot_t(reader, coef), 0.0)
-            inflow = inflow + jnp.where(ahead, entry[first], entry[first + 1]) * dot(
-                scores, driven
-            )
+            out.append((q, jnp.where(ahead, totals_f[m], totals_b[m]), dot(scores, driven)))
+        return out
+
+    def decayed(first, place, parts):
+        exponents = []
+        for q, _, _ in parts:
+            exponent = jnp.where(q < place, entry[first], entry[first + 1])
+            for other, between, _ in parts:
+                inner_f = (q < other) & (other < place)
+                inner_b = (q > other) & (other > place)
+                exponent = exponent + jnp.where(inner_f | inner_b, between, 0.0)
+            exponents.append(exponent)
+        wide = dot_first(jnp.exp(jnp.concatenate(exponents, axis=1)), expand)
+        inflow = jnp.zeros((cells, inner), F32)
+        for m, (_, _, part) in enumerate(parts):
+            inflow = inflow + wide[m * cells : (m + 1) * cells] * part
         return inflow
 
     for copy in hz_copies:
@@ -458,10 +455,18 @@
         passed[e + 1].start()
     for copy in col_copies:
         copy.wait()
-    total = total + entering(2, strip_col, hz_col, r, n_row, j0 == j1, i0 - i1)
-    for copy in passed:
+    others_r = [lax.rem(r + n_row - o, n_row) for o in range(1, n_row)]
+    total = total + decayed(
+        2, r, entering(2, strip_col, hz_col, r, others_r, j0 == j1, i0 - i1)
+    )
+    passed[0].wait()
+    near = [sibling] + [lax.rem(c + n_col - o, n_col) for o in range(2, n_col, 2)]
+    far = [lax.rem(sibling + n_col - o, n_col) for o in range(2, n_col, 2)]
+    parts = entering(0, strip_row, hz_row, c, near, i0 == i1, j0 - j1)
+    for copy in passed[1:]:
         copy.wait()
-    total = total + entering(0, strip_row, hz_row, c, n_col, i0 == i1, j0 - j1)
+    parts += entering(0, strip_row, hz_row, c, far, i0 == i1, j0 - j1)
+    total = total + decayed(0, c, parts)
 
     loads[13].wait()
     loads[14].wait()
@@ -541,8 +546,8 @@
             pltpu.VMEM((n_row, 1, cells), F32),
             pltpu.VMEM((n_col, cells, inner), BF16),
             pltpu.VMEM((n_row, cells, inner), BF16),
-            dma((count,)),
-            dma((count,)),
+            dma,
+            dma,
             dma((10,)),
             dma((10,)),
             dma((n_col,)),

time: 26.7 us -> 25.8 us (0.966)
  Pallas kernels: 25 us -> 24.2 us
    pallas_call x1, Pallas kernels: 25 us -> 24.2 us  [per_device(): pl.pallas_call(functools.partial(kernel, n_row, n_col), out_shape=jax.Sha...]
where the time goes in v1:
time: 25.8 us; the launch traced here: 25.6 us
  Pallas kernels  24.2 us (94%)
  local copies, waits for them, and re-layouts  1.47 us (6%)
    pallas_call x1, Pallas kernels, per_device(): pl.pallas_call(functools.partial(kernel, n_row, n_col), out_shape=jax.Sha...  24.2 us
    unnamed x1, local copies, waits for them, and re-layouts  1.47 us

profile of v1, /device:TPU:0, one launch (start us, length us, event | category | flops | bytes accessed | tf_op | source)
XLA Modules:
  0.0 25.6 jit_solution(14540596620402317416)
XLA Ops:
  0.0 24.2 %shard_map.145 = bf16[16,8,256]{2,1,0:T(8,128)(2,1)} custom-call(bf16[16,8,256]{2,1,0:T(8,128)(2,1)} %refs_0_.1, bf16[1,256]{1,0:T(2,128)(2,1)} %refs_1_.1, bf16[256,256]{1,0:T(8,128)(2,1)} %refs_2_.1, s32[8]{0:T(128)} %refs_3_.1, f32[1,256]{1,0:T(1,128)} %bitcast.6, bf16[256,512]{1,0:T(8,128)(2,1)} %refs_5_.1, f32[9,256]{1,0:T(8,128)} %refs_6_.1, ...), custom_call_target="tpu_custom_call" | custom-call | tf_op jit(solution)/shard_map/pallas_call | solution.py:527
  24.2 1.5 %copy.17 = bf16[16,8,256]{2,1,0:T(8,128)(2,1)} copy(bf16[16,8,256]{2,1,0:T(8,128)(2,1)} %shard_map.145) | data formatting | bytes 131072
